TPU v7x, 32 devices: a whole 2x2x4 slice. The times are simulated.
32 devices in a mesh: region: 2 (over y), rows: 16 (over z, x, core).
Axes of the slice: x: 2, y: 2, z: 4, core: 2. Of those that a mesh axis runs over, the one named last changes fastest.
Arguments:
- features: bfloat16 [20480, 768], P(('region', 'rows')), parts along dimension 0
- seed_labels: int32 [20480], P(('region', 'rows')), parts along dimension 0, may hold values from -1 to 1023, as said below
- neighbours: int32 [160, 16], P(('region', 'rows')), parts along dimension 0, may hold values from 0 to 79, as said below
- hub_blocks: int32 [8], P('region'), parts along dimension 0, may hold values from 0 to 79, as said below
Outputs:
- scores: float32 [20480, 1024], P(('region', 'rows')), parts along dimension 0
There are 2 independent parts, one for each index of `region`. A program takes and returns all parts, laid end to end along the dimension named above; each array names one. Nothing has to cross between parts.
Inputs may be any that keep to these rules, and one draw needn't show every extreme that they name: `seed_labels`: each block of 128 crops holds at least two labelled crops. `neighbours`: slot 0 of block b is b itself; the other slots name distinct blocks at most 10 blocks away from b along the closed loop of the 80 blocks (b - 1 and b + 1 beside it, 0 beside 80 - 1). `hub_blocks`: the hub ids are distinct, and one of them is 79.
All inputs are finite; a program needn't handle non-finite values.
Results may differ from a plain program's by a relative error of at most 0.00095.
Values may be sent and summed in bfloat16 or wider, within the bound.
A program may use at most 128 MiB of HBM per device.

v0:
```python
import jax
import jax.numpy as jnp
from jax import lax
from jax.sharding import PartitionSpec as P

C = 1024
ITERS = 3


spread_rate = 0.9
kernel_width = 0.25
epsilon = 1e-06


def from_behind(value, axis, steps):
    count = lax.axis_size(axis)
    pairs = [(source, (source + steps) % count) for source in range(count)]
    return lax.ppermute(value, axis, pairs)


def spread_2(block, axis, owner):
    block = jnp.where(lax.axis_index(axis) == owner, block, jnp.zeros_like(block))
    return lax.psum(block, axis)


def unit_rows(features):
    values = features.astype(jnp.float32)
    scaled = values * lax.rsqrt(jnp.mean(values * values, axis=1, keepdims=True) + epsilon)
    return (scaled * features.shape[1] ** (-0.5)).astype(jnp.bfloat16)


def window_features(blocks):
    pieces = {}
    for offset in (2, 1, -1, -2):
        pieces[offset] = from_behind(blocks, "rows", offset)
    return jnp.concatenate([pieces[2], pieces[1], blocks, pieces[-1], pieces[-2]], axis=0)


def window_labels(blocks):
    pieces = {}
    for offset in (2, 1, -1, -2):
        pieces[offset] = from_behind(blocks, "rows", offset)
    return jnp.concatenate([pieces[2], pieces[1], blocks, pieces[-1], pieces[-2]], axis=0)


def hub_features(blocks, owners, places):
    return jnp.stack(
        [
            spread_2(blocks[places[number]], "rows", owners[number])
            for number in range(owners.shape[0])
        ],
        axis=0,
    )


def hub_labels(blocks, owners, places):
    return jnp.stack(
        [
            spread_2(blocks[places[number]], "rows", owners[number])
            for number in range(owners.shape[0])
        ],
        axis=0,
    )


def on_device(features, seed_labels, neighbours, hub_blocks):
    device = lax.axis_index("rows")
    devices = lax.axis_size("rows")
    block_count = neighbours.shape[0]
    block_rows = features.shape[0] // block_count
    window_slots = neighbours.shape[1]
    hub_count = hub_blocks.shape[0]
    slots = window_slots + hub_count
    all_blocks = devices * block_count
    reach = 2 * block_count
    local_ids = device * block_count + jnp.arange(block_count, dtype=jnp.int32)
    distance = (neighbours - local_ids[:, None]) % all_blocks
    distance = jnp.where(distance > all_blocks // 2, distance - all_blocks, distance)
    window_index = jnp.arange(block_count, dtype=jnp.int32)[:, None] + reach + distance
    hub_index = jnp.broadcast_to(
        5 * block_count + jnp.arange(hub_count, dtype=jnp.int32)[None, :], (block_count, hub_count)
    )
    table_index = jnp.concatenate([window_index, hub_index], axis=1)
    listed = jnp.concatenate(
        [neighbours, jnp.broadcast_to(hub_blocks[None, :], (block_count, hub_count))], axis=1
    )
    owners = hub_blocks // block_count
    places = hub_blocks % block_count
    unit = unit_rows(features).reshape(block_count, block_rows, features.shape[1])
    feature_table = jnp.concatenate(
        [window_features(unit), hub_features(unit, owners, places)], axis=0
    )
    line = jnp.arange(block_rows, dtype=jnp.int32)
    diagonal_mask = line[:, None] == line[None, :]

    def weigh(packed):
        own_rows, index_row, neighbour_row, block_id = packed
        kernels = []
        degree = jnp.zeros((block_rows,), jnp.float32)
        for slot in range(slots):
            slab = lax.dynamic_index_in_dim(feature_table, index_row[slot], 0, keepdims=False)
            dots = lax.dot_general(
                own_rows, slab, (((1,), (1,)), ((), ())), preferred_element_type=jnp.float32
            )
            kernel = jnp.exp((dots - 1.0) / kernel_width)
            same_crop = diagonal_mask & (neighbour_row[slot] == block_id)
            kernel = jnp.where(same_crop, jnp.float32(0.0), kernel)
            degree = degree + jnp.sum(kernel, axis=1)
            kernels.append(kernel.astype(jnp.bfloat16))
        return (jnp.concatenate(kernels, axis=1), degree)

    weights, degree = lax.map(weigh, (unit, table_index, listed, local_ids))
    inverse_root = lax.rsqrt(degree).reshape(block_count * block_rows, 1)
    seeds = (seed_labels[:, None] == jnp.arange(C, dtype=jnp.int32)[None, :]).astype(jnp.float32)
    spread = seeds
    for iteration in range(ITERS):
        scaled = (inverse_root * spread).astype(jnp.bfloat16).reshape(block_count, block_rows, C)
        label_table = jnp.concatenate(
            [window_labels(scaled), hub_labels(scaled, owners, places)], axis=0
        )

        def apply(packed):
            block_weights, index_row = packed
            total = jnp.zeros((block_rows, C), jnp.float32)
            for slot in range(slots):
                slab = lax.dynamic_index_in_dim(label_table, index_row[slot], 0, keepdims=False)
                part_weights = block_weights[:, slot * block_rows : (slot + 1) * block_rows]
                total = total + jnp.dot(part_weights, slab, preferred_element_type=jnp.float32)
            return total

        gathered_sum = lax.map(apply, (weights, table_index)).reshape(block_count * block_rows, C)
        spread = spread_rate * inverse_root * gathered_sum + (1.0 - spread_rate) * seeds
    totals = jnp.sum(spread, axis=1, keepdims=True)
    return jnp.log(1.0 + C * spread / totals)


def solution(mesh):
    placed = (
        P(("region", "rows"), None),
        P(("region", "rows")),
        P(("region", "rows"), None),
        P("region"),
    )
    return jax.shard_map(
        on_device,
        mesh=mesh,
        in_specs=placed,
        out_specs=P(("region", "rows"), None),
        check_vma=False,
    )
```

profile of v0, /device:TPU:1, one launch (start us, length us, event | category | flops | bytes accessed | tf_op | source)
XLA Modules:
  0.0 1978.7 jit_solution(3695934678606668636)
XLA Ops:
  13.7 2.9 collective-permute-start.3
  31.3 34.6 %collective-permute-done = bf16[5,128,768]{2,1,0:T(8,128)(2,1)} collective-permute-done((bf16[5,128,768]{2,1,0:T(8,128)(2,1)S(1)}, bf16[5,128,768]{2,1,0:T(8,128)(2,1)}, u32[]{:S(2)}, u32[]{:S(2)}) %collective-permute-start) | collective-permute-done | bytes 983072 | tf_op jit(solution)/shard_map/ppermute | solution.py:18
  68.1 10.2 collective-permute-done.1
  83.6 51.2 %all-reduce.15.cloned.1.call-done = (bf16[1,128,768]{2,1,0:T(8,128)(2,1)}, bf16[1,128,768]{2,1,0:T(8,128)(2,1)}, bf16[1,128,768]{2,1,0:T(8,128)(2,1)}, bf16[1,128,768]{2,1,0:T(8,128)(2,1)}) async-done(((bf16[1,128,768]{2,1,0:T(8,128)(2,1)}, bf16[1,128,768]{2,1,0:T(8,128)(2,1)}, bf16[1,128,768]{2,1,0:T(8,128)(2,1)}, bf16[1,128,768]{2,1,0:T(8,128)(2,1)}), (bf16[1,128,768]{2,1,0:T(8,128)(2,1)}, ...) | async-done | bytes 786448 | tf_op jit(solution)/shard_map/psum | solution.py:23
  141.3 452.1 %while.50 = (s32[]{:T(128)}, bf16[5,128,2560]{2,1,0:T(8,128)(2,1)}, f32[5,128]{1,0:T(8,128)S(1)}, s32[5,20]{1,0:T(8,128)S(1)}, s32[5]{0:T(128)S(1)}, /*index=5*/...) while((s32[]{:T(128)}, bf16[5,128,2560]{2,1,0:T(8,128)(2,1)}, ...), condition=%wide.region_26.27_spmd.clone.clone, body=%wide.region_5.26_spmd.clone.clone.sunk | while | flops 505610112 | bytes 13797129 | solution.py:112
  594.1 3.7 collective-permute-start.5
  597.8 3.1 collective-permute-start.7
  602.0 62.9 %collective-permute-done.4 = bf16[5,128,1024]{2,1,0:T(8,128)(2,1)} collective-permute-done((bf16[5,128,1024]{2,1,0:T(8,128)(2,1)S(1)}, bf16[5,128,1024]{2,1,0:T(8,128)(2,1)}, u32[]{:S(2)}, u32[]{:S(2)}) %collective-permute-start.4) | collective-permute-done | bytes 1310752 | tf_op jit(solution)/shard_map/ppermute | solution.py:18
  667.4 15.3 collective-permute-done.5
  682.8 2.5 constant_dynamic-update-slice_fusion.36
  686.7 2.5 constant_dynamic-update-slice_fusion.35
  690.4 40.2 %all-reduce.13.cloned.1.call-done = (bf16[1,128,1024]{2,1,0:T(8,128)(2,1)}, bf16[1,128,1024]{2,1,0:T(8,128)(2,1)}, bf16[1,128,1024]{2,1,0:T(8,128)(2,1)}, bf16[1,128,1024]{2,1,0:T(8,128)(2,1)}) async-done(((bf16[1,128,1024]{2,1,0:T(8,128)(2,1)}, bf16[1,128,1024]{2,1,0:T(8,128)(2,1)}, bf16[1,128,1024]{2,1,0:T(8,128)(2,1)}, bf16[1,128,1024]{2,1,0:T(8,128)(2,1)}), (bf16[1,128,1024]{2,1,0:T(8,128)(2,1)}, ...) | async-done | bytes 1048592 | tf_op jit(solution)/shard_map/psum | solution.py:23
  739.2 310.7 %while.47 = (s32[]{:T(128)}, f32[5,128,1024]{2,1,0:T(8,128)}, bf16[5,128,2560]{2,1,0:T(8,128)(2,1)}, s32[5,20]{1,0:T(8,128)S(1)}, bf16[29,128,1024]{2,1,0:T(8,128)(2,1)}, /*index=5*/s32[]{:T(128)}, s32[]{:T(128)}, s32[]{:T(128)}) while((s32[]{:T(128)}, f32[5,128,1024]{2,1,0:T(8,128)}, bf16[5,128,2560]{2,1,0:T(8,128)(2,1)}, ...), condition=%wide.region_32.33_spmd, body=%wide.region_31.32_spmd.sunk | while | flops 673579008 | bytes 30279316 | solution.py:131
  1049.9 3.6 fusion.412
  1053.8 3.8 collective-permute-start.9
  1057.6 2.6 collective-permute-start.11
  1062.4 62.9 %collective-permute-done.8 = bf16[5,128,1024]{2,1,0:T(8,128)(2,1)} collective-permute-done((bf16[5,128,1024]{2,1,0:T(8,128)(2,1)}, bf16[5,128,1024]{2,1,0:T(8,128)(2,1)}, u32[]{:S(2)}, u32[]{:S(2)}) %collective-permute-start.8) | collective-permute-done | bytes 1310752 | tf_op jit(solution)/shard_map/ppermute | solution.py:18
  1127.8 14.9 collective-permute-done.9
  1146.9 2.5 constant_dynamic-update-slice_fusion.43
  1149.5 2.6 constant_dynamic-update-slice_fusion.42
  1152.1 38.5 %all-reduce.11.cloned.1.call-done = (bf16[1,128,1024]{2,1,0:T(8,128)(2,1)}, bf16[1,128,1024]{2,1,0:T(8,128)(2,1)}, bf16[1,128,1024]{2,1,0:T(8,128)(2,1)}, bf16[1,128,1024]{2,1,0:T(8,128)(2,1)}) async-done(((bf16[1,128,1024]{2,1,0:T(8,128)(2,1)}, bf16[1,128,1024]{2,1,0:T(8,128)(2,1)}, bf16[1,128,1024]{2,1,0:T(8,128)(2,1)}, bf16[1,128,1024]{2,1,0:T(8,128)(2,1)}), (bf16[1,128,1024]{2,1,0:T(8,128)(2,1)}, ...) | async-done | bytes 1048592 | tf_op jit(solution)/shard_map/psum | solution.py:23
  1199.1 310.7 %while.48 = (s32[]{:T(128)}, f32[5,128,1024]{2,1,0:T(8,128)}, bf16[5,128,2560]{2,1,0:T(8,128)(2,1)}, s32[5,20]{1,0:T(8,128)S(1)}, bf16[29,128,1024]{2,1,0:T(8,128)(2,1)}, /*index=5*/s32[]{:T(128)}, s32[]{:T(128)}, s32[]{:T(128)}) while((s32[]{:T(128)}, f32[5,128,1024]{2,1,0:T(8,128)}, bf16[5,128,2560]{2,1,0:T(8,128)(2,1)}, ...), condition=%wide.region_38.39_spmd, body=%wide.region_37.38_spmd.sunk | while | flops 673579008 | bytes 30279316 | solution.py:131
  1509.8 3.6 fusion.414
  1513.7 3.8 collective-permute-start.13
  1517.5 2.6 collective-permute-start.15
  1522.2 62.9 %collective-permute-done.12 = bf16[5,128,1024]{2,1,0:T(8,128)(2,1)} collective-permute-done((bf16[5,128,1024]{2,1,0:T(8,128)(2,1)}, bf16[5,128,1024]{2,1,0:T(8,128)(2,1)}, u32[]{:S(2)}, u32[]{:S(2)}) %collective-permute-start.12) | collective-permute-done | bytes 1310752 | tf_op jit(solution)/shard_map/ppermute | solution.py:18
  1587.7 14.9 collective-permute-done.13
  1606.8 2.5 constant_dynamic-update-slice_fusion.52
  1609.4 2.6 constant_dynamic-update-slice_fusion.51
  1612.0 38.5 %all-reduce.9.cloned.1.call-done = (bf16[1,128,1024]{2,1,0:T(8,128)(2,1)}, bf16[1,128,1024]{2,1,0:T(8,128)(2,1)}, bf16[1,128,1024]{2,1,0:T(8,128)(2,1)}, bf16[1,128,1024]{2,1,0:T(8,128)(2,1)}) async-done(((bf16[1,128,1024]{2,1,0:T(8,128)(2,1)}, bf16[1,128,1024]{2,1,0:T(8,128)(2,1)}, bf16[1,128,1024]{2,1,0:T(8,128)(2,1)}, bf16[1,128,1024]{2,1,0:T(8,128)(2,1)}), (bf16[1,128,1024]{2,1,0:T(8,128)(2,1)}, ...) | async-done | bytes 1048592 | tf_op jit(solution)/shard_map/psum | solution.py:23
  1659.1 307.3 %while.49 = (s32[]{:T(128)}, f32[5,128,1024]{2,1,0:T(8,128)}, bf16[5,128,2560]{2,1,0:T(8,128)(2,1)}, s32[5,20]{1,0:T(8,128)S(1)}, bf16[29,128,1024]{2,1,0:T(8,128)(2,1)}, /*index=5*/s32[]{:T(128)}, s32[]{:T(128)}, s32[]{:T(128)}) while((s32[]{:T(128)}, f32[5,128,1024]{2,1,0:T(8,128)}, bf16[5,128,2560]{2,1,0:T(8,128)(2,1)}, ...), condition=%wide.region_44.45_spmd, body=%wide.region_43.44_spmd.sunk | while | flops 673579008 | bytes 30279316 | solution.py:131
  1968.7 3.4 fusion.420
  (702 shorter events, 623.4 us)
Async XLA Ops:
  6.5 128.3 %all-reduce.15.cloned.1.call-start = ((), (), s32[]{:S(2)}) async-start(), calls=%async_computation.3 | async-start | bytes 1572864 | tf_op jit(solution)/shard_map/psum | solution.py:23
  9.5 74.1 %copy-start = (bf16[640,768]{1,0:T(8,128)(2,1)}, bf16[640,768]{1,0:T(8,128)(2,1)S(1)}, u32[]{:S(2)}) copy-start(bf16[640,768]{1,0:T(8,128)(2,1)S(1)} %fusion.423) | copy-start | bytes 2949124
  9.5 56.4 %collective-permute-start = (bf16[5,128,768]{2,1,0:T(8,128)(2,1)S(1)}, bf16[5,128,768]{2,1,0:T(8,128)(2,1)}, u32[]{:S(2)}, u32[]{:S(2)}) collective-permute-start(bf16[5,128,768]{2,1,0:T(8,128)(2,1)S(1)} %bitcast.957), channel_id=1, source_target_pairs={{0,2},{1,3},{2,4},{3,5},{4,6},{5,7},{6,8},{7,9},{8,10},{9,11},{10,... | collective-permute-start | bytes 2949128 | tf_op jit(solution)/shard_map/ppermute | solution.py:18
  11.6 66.6 %collective-permute-start.1 = (bf16[5,128,768]{2,1,0:T(8,128)(2,1)S(1)}, bf16[5,128,768]{2,1,0:T(8,128)(2,1)}, u32[]{:S(2)}, u32[]{:S(2)}) collective-permute-start(bf16[5,128,768]{2,1,0:T(8,128)(2,1)S(1)} %bitcast.958), channel_id=1, source_target_pairs={{0,1},{1,2},{2,3},{3,4},{4,5},{5,6},{6,7},{7,8},{8,9},{9,10},{10,1... | collective-permute-start | bytes 2949128 | tf_op jit(solution)/shard_map/ppermute | solution.py:18
  13.7 67.8 %collective-permute-start.2 = (bf16[5,128,768]{2,1,0:T(8,128)(2,1)S(1)}, bf16[5,128,768]{2,1,0:T(8,128)(2,1)S(1)}, u32[]{:S(2)}, u32[]{:S(2)}) collective-permute-start(bf16[5,128,768]{2,1,0:T(8,128)(2,1)S(1)} %bitcast.959), channel_id=1, source_target_pairs={{0,15},{1,0},{2,1},{3,2},{4,3},{5,4},{6,5},{7,6},{8,7},{9,8},{10,9... | collective-permute-start | bytes 2949128 | tf_op jit(solution)/shard_map/ppermute | solution.py:18
  13.7 68.8 %collective-permute-start.3 = (bf16[5,128,768]{2,1,0:T(8,128)(2,1)S(1)}, bf16[5,128,768]{2,1,0:T(8,128)(2,1)S(1)}, u32[]{:S(2)}, u32[]{:S(2)}) collective-permute-start(bf16[5,128,768]{2,1,0:T(8,128)(2,1)S(1)} %bitcast.960), channel_id=1, source_target_pairs={{0,14},{1,15},{2,0},{3,1},{4,2},{5,3},{6,4},{7,5},{8,6},{9,7},{10,... | collective-permute-start | bytes 2949128 | tf_op jit(solution)/shard_map/ppermute | solution.py:18
  28.9 701.7 %all-reduce.13.cloned.1.call-start = ((), (), s32[]{:S(2)}) async-start(), calls=%async_computation.2 | async-start | bytes 2097152 | tf_op jit(solution)/shard_map/psum | solution.py:23
  141.3 452.1 %copy-start.6 = (s32[640]{0:T(1024)S(1)}, s32[640]{0:T(1024)}, u32[]{:S(2)}) copy-start(s32[640]{0:T(1024)} %param.13) | copy-start | bytes 7684
  593.7 71.2 %collective-permute-start.4 = (bf16[5,128,1024]{2,1,0:T(8,128)(2,1)S(1)}, bf16[5,128,1024]{2,1,0:T(8,128)(2,1)}, u32[]{:S(2)}, u32[]{:S(2)}) collective-permute-start(bf16[5,128,1024]{2,1,0:T(8,128)(2,1)S(1)} %select_convert_fusion), channel_id=1, source_target_pairs={{0,2},{1,3},{2,4},{3,5},{4,6},{5,7},{6,8},{7,9},{8,10},{9,11},{10,... | collective-permute-start | bytes 3932168 | tf_op jit(solution)/shard_map/ppermute | solution.py:18
  594.1 88.6 %collective-permute-start.5 = (bf16[5,128,1024]{2,1,0:T(8,128)(2,1)S(1)}, bf16[5,128,1024]{2,1,0:T(8,128)(2,1)}, u32[]{:S(2)}, u32[]{:S(2)}) collective-permute-start(bf16[5,128,1024]{2,1,0:T(8,128)(2,1)S(1)} %select_convert_fusion), channel_id=1, source_target_pairs={{0,1},{1,2},{2,3},{3,4},{4,5},{5,6},{6,7},{7,8},{8,9},{9,10},{10,1... | collective-permute-start | bytes 3932168 | tf_op jit(solution)/shard_map/ppermute | solution.py:18
  597.8 88.9 %collective-permute-start.6 = (bf16[5,128,1024]{2,1,0:T(8,128)(2,1)S(1)}, bf16[5,128,1024]{2,1,0:T(8,128)(2,1)}, u32[]{:S(2)}, u32[]{:S(2)}) collective-permute-start(bf16[5,128,1024]{2,1,0:T(8,128)(2,1)S(1)} %select_convert_fusion), channel_id=1, source_target_pairs={{0,15},{1,0},{2,1},{3,2},{4,3},{5,4},{6,5},{7,6},{8,7},{9,8},{10,9... | collective-permute-start | bytes 3932168 | tf_op jit(solution)/shard_map/ppermute | solution.py:18
  597.8 91.4 %collective-permute-start.7 = (bf16[5,128,1024]{2,1,0:T(8,128)(2,1)S(1)}, bf16[5,128,1024]{2,1,0:T(8,128)(2,1)S(1)}, u32[]{:S(2)}, u32[]{:S(2)}) collective-permute-start(bf16[5,128,1024]{2,1,0:T(8,128)(2,1)S(1)} %select_convert_fusion), channel_id=1, source_target_pairs={{0,14},{1,15},{2,0},{3,1},{4,2},{5,3},{6,4},{7,5},{8,6},{9,7},{10,... | collective-permute-start | bytes 3932168 | tf_op jit(solution)/shard_map/ppermute | solution.py:18
  601.9 588.7 %all-reduce.11.cloned.1.call-start = ((), (), s32[]{:S(2)}) async-start(), calls=%async_computation.1 | async-start | bytes 2097152 | tf_op jit(solution)/shard_map/psum | solution.py:23
  742.9 4.3 copy-start.1
  805.0 4.3 copy-start.1
  867.2 4.3 copy-start.1
  1049.9 95.4 %copy-start.4 = (f32[5,128,1024]{2,1,0:T(8,128)S(1)}, f32[5,128,1024]{2,1,0:T(8,128)}, u32[]{:S(2)}) copy-start(f32[5,128,1024]{2,1,0:T(8,128)} %get-tuple-element.301) | copy-start | bytes 7864324
  1053.5 71.8 %collective-permute-start.8 = (bf16[5,128,1024]{2,1,0:T(8,128)(2,1)}, bf16[5,128,1024]{2,1,0:T(8,128)(2,1)}, u32[]{:S(2)}, u32[]{:S(2)}) collective-permute-start(bf16[5,128,1024]{2,1,0:T(8,128)(2,1)} %fusion.412), channel_id=1, source_target_pairs={{0,2},{1,3},{2,4},{3,5},{4,6},{5,7},{6,8},{7,9},{8,10},{9,11},{10,... | collective-permute-start | bytes 3932168 | tf_op jit(solution)/shard_map/ppermute | solution.py:18
  1053.8 88.9 %collective-permute-start.9 = (bf16[5,128,1024]{2,1,0:T(8,128)(2,1)}, bf16[5,128,1024]{2,1,0:T(8,128)(2,1)}, u32[]{:S(2)}, u32[]{:S(2)}) collective-permute-start(bf16[5,128,1024]{2,1,0:T(8,128)(2,1)} %fusion.412), channel_id=1, source_target_pairs={{0,1},{1,2},{2,3},{3,4},{4,5},{5,6},{6,7},{7,8},{8,9},{9,10},{10,1... | collective-permute-start | bytes 3932168 | tf_op jit(solution)/shard_map/ppermute | solution.py:18
  1057.6 89.4 %collective-permute-start.10 = (bf16[5,128,1024]{2,1,0:T(8,128)(2,1)}, bf16[5,128,1024]{2,1,0:T(8,128)(2,1)}, u32[]{:S(2)}, u32[]{:S(2)}) collective-permute-start(bf16[5,128,1024]{2,1,0:T(8,128)(2,1)} %fusion.412), channel_id=1, source_target_pairs={{0,15},{1,0},{2,1},{3,2},{4,3},{5,4},{6,5},{7,6},{8,7},{9,8},{10,9... | collective-permute-start | bytes 3932168 | tf_op jit(solution)/shard_map/ppermute | solution.py:18
  1057.6 91.9 %collective-permute-start.11 = (bf16[5,128,1024]{2,1,0:T(8,128)(2,1)}, bf16[5,128,1024]{2,1,0:T(8,128)(2,1)}, u32[]{:S(2)}, u32[]{:S(2)}) collective-permute-start(bf16[5,128,1024]{2,1,0:T(8,128)(2,1)} %fusion.412), channel_id=1, source_target_pairs={{0,14},{1,15},{2,0},{3,1},{4,2},{5,3},{6,4},{7,5},{8,6},{9,7},{10,... | collective-permute-start | bytes 3932168 | tf_op jit(solution)/shard_map/ppermute | solution.py:18
  1062.4 588.1 %all-reduce.9.cloned.1.call-start = ((), (), s32[]{:S(2)}) async-start(), calls=%async_computation | async-start | bytes 2097152 | tf_op jit(solution)/shard_map/psum | solution.py:23
  1509.8 95.4 %copy-start.5 = (f32[5,128,1024]{2,1,0:T(8,128)S(1)}, f32[5,128,1024]{2,1,0:T(8,128)}, u32[]{:S(2)}) copy-start(f32[5,128,1024]{2,1,0:T(8,128)} %get-tuple-element.302) | copy-start | bytes 7864324
  1513.4 71.8 %collective-permute-start.12 = (bf16[5,128,1024]{2,1,0:T(8,128)(2,1)}, bf16[5,128,1024]{2,1,0:T(8,128)(2,1)}, u32[]{:S(2)}, u32[]{:S(2)}) collective-permute-start(bf16[5,128,1024]{2,1,0:T(8,128)(2,1)} %fusion.414), channel_id=1, source_target_pairs={{0,2},{1,3},{2,4},{3,5},{4,6},{5,7},{6,8},{7,9},{8,10},{9,11},{10,... | collective-permute-start | bytes 3932168 | tf_op jit(solution)/shard_map/ppermute | solution.py:18
  1513.7 88.9 %collective-permute-start.13 = (bf16[5,128,1024]{2,1,0:T(8,128)(2,1)}, bf16[5,128,1024]{2,1,0:T(8,128)(2,1)}, u32[]{:S(2)}, u32[]{:S(2)}) collective-permute-start(bf16[5,128,1024]{2,1,0:T(8,128)(2,1)} %fusion.414), channel_id=1, source_target_pairs={{0,1},{1,2},{2,3},{3,4},{4,5},{5,6},{6,7},{7,8},{8,9},{9,10},{10,1... | collective-permute-start | bytes 3932168 | tf_op jit(solution)/shard_map/ppermute | solution.py:18
  1517.5 89.4 %collective-permute-start.14 = (bf16[5,128,1024]{2,1,0:T(8,128)(2,1)}, bf16[5,128,1024]{2,1,0:T(8,128)(2,1)}, u32[]{:S(2)}, u32[]{:S(2)}) collective-permute-start(bf16[5,128,1024]{2,1,0:T(8,128)(2,1)} %fusion.414), channel_id=1, source_target_pairs={{0,15},{1,0},{2,1},{3,2},{4,3},{5,4},{6,5},{7,6},{8,7},{9,8},{10,9... | collective-permute-start | bytes 3932168 | tf_op jit(solution)/shard_map/ppermute | solution.py:18
  1517.5 91.9 %collective-permute-start.15 = (bf16[5,128,1024]{2,1,0:T(8,128)(2,1)}, bf16[5,128,1024]{2,1,0:T(8,128)(2,1)}, u32[]{:S(2)}, u32[]{:S(2)}) collective-permute-start(bf16[5,128,1024]{2,1,0:T(8,128)(2,1)} %fusion.414), channel_id=1, source_target_pairs={{0,14},{1,15},{2,0},{3,1},{4,2},{5,3},{6,4},{7,5},{8,6},{9,7},{10,... | collective-permute-start | bytes 3932168 | tf_op jit(solution)/shard_map/ppermute | solution.py:18
  1662.9 4.7 copy-start.3
  1724.3 4.7 copy-start.3
  1785.8 4.7 copy-start.3
  1847.2 4.7 copy-start.3
  1908.7 4.7 copy-start.3
  (7 other events, 30.0 us)
Sparse Core Ops, SparseCore 0:
  29.1 105.6 all-reduce.14
  602.0 128.5 all-reduce.12
  1062.5 128.0 all-reduce.10
  1522.4 128.0 all-reduce.8
where the time goes:
time: 2000 us; the launch traced here: 1980 us
  loops' own time  837 us (42%)
  matrix products  496 us (25%)
  waiting for transfers between devices  447 us (22%)
  local copies, waits for them, and re-layouts  115 us (6%)
  other arithmetic  32.7 us (2%)
  starting transfers between devices  27.8 us (1%)
  between operations  23.2 us (1%)
    another operation x3, loops' own time, on_device(): lax.map(apply, (weights, table_index)).reshape(block_count * block_rows, C)  530 us
    dot_general x300, matrix products, apply(): jnp.dot(part_weights, slab, preferred_element_type=jnp.float32)  370 us
    another operation x1, loops' own time, on_device(): weights, degree = lax.map(weigh, (unit, table_index, listed, local_ids))  306 us
    ppermute x16, waiting for transfers between devices, from_behind(): return lax.ppermute(value, axis, pairs)  279 us
    psum x4, waiting for transfers between devices, spread_2(): return lax.psum(block, axis)  168 us
    dot_general x100, matrix products, weigh(): lax.dot_general(own_rows, slab, (((1,), (1,)), ((), ())), preferred_eleme...  126 us
    unnamed x37, local copies, waits for them, and re-layouts  56.7 us
  transfers between devices with their start and end apart: 20, of which 12 were waited for; matrix products, arithmetic and copies ran while one was open for 3% of the time, Pallas kernels for 0%

commit v1 on v0

v1 whole, which is shorter than its diff:
```python
import functools
import math

import jax
import jax.numpy as jnp
from jax import lax
from jax.experimental import pallas as pl
from jax.experimental.pallas import tpu as pltpu
from jax.sharding import PartitionSpec as P

ITERS = 3
GROUP = 4
LOG2E = math.log2(math.e)

spread_rate = 0.9
kernel_width = 0.25
epsilon = 1e-06


def kernel(groups, blk, cols, feat_ref, meta_ref, hub_ref, out_ref,
           table, weights, labels, inv_root, label_col, meta, bias,
           hub_send, hub_recv, lab_send, lab_recv, res, res_half, from_sib, from_x, from_d, pick,
           f_send, f_recv, m_send, m_recv, h_send, h_recv, p_send, p_recv,
           z_send, z_recv, l_send, l_recv, r_send, r_recv):
    own_blocks = feat_ref.shape[0] // blk
    width = feat_ref.shape[1]
    reach = 2 * own_blocks
    group_blocks = GROUP * own_blocks
    window = group_blocks + 2 * reach
    hubs = GROUP
    pairs = group_blocks // 2
    span = (2 * reach + 2) * blk
    quarter = cols // GROUP
    stages = groups.bit_length() - 1

    me = lax.axis_index("rows")
    g, q = lax.div(me, GROUP), lax.rem(me, GROUP)
    c, x = lax.rem(q, 2), lax.div(q, 2)
    q_sib = q + 1 - 2 * c
    q_x = q + 2 - 4 * x
    q_d = q_x + 1 - 2 * c
    sib, xp, dp = g * GROUP + q_sib, g * GROUP + q_x, g * GROUP + q_d
    up = lax.rem(g + 1, groups) * GROUP + q
    down = lax.rem(g + groups - 1, groups) * GROUP + q
    first = x * up + (1 - x) * down
    second = x * down + (1 - x) * up
    partners = []
    for s in range(stages):
        size = 2 ** (s + 1)
        pg = lax.div(g, size) * size + size - 1 - lax.rem(g, size)
        partners.append(pg * GROUP + q)

    def remote(src, dst, send, recv, device):
        return pltpu.make_async_remote_copy(
            src_ref=src, dst_ref=dst, send_sem=send, recv_sem=recv,
            device_id={"rows": device}, device_id_type=pl.DeviceIdType.MESH)

    barrier = pltpu.get_barrier_semaphore()
    everyone = [sib, xp, dp, up, down] + partners
    for device in everyone:
        pl.semaphore_signal(barrier, inc=1, device_id={"rows": device},
                            device_id_type=pl.DeviceIdType.MESH)
    pl.semaphore_wait(barrier, len(everyone))

    pending = []

    def at(position):
        return pl.ds(pl.multiple_of(position * blk, blk), blk)

    meta[q] = meta_ref[...]
    meta_copies = []
    for k, device in enumerate((sib, xp, dp)):
        copy = remote(meta.at[q], meta.at[q], m_send.at[k], m_recv.at[k], device)
        copy.start()
        meta_copies.append(copy)

    pos_a = reach + own_blocks * q
    pos_b = reach + own_blocks * q_x
    edge = reach + group_blocks
    dst_a = x * (own_blocks * c) + (1 - x) * (edge + own_blocks * c)
    dst_b = (1 - x) * (own_blocks * c) + x * (edge + own_blocks * c)

    def fcopy(kind, n, src, dst, device):
        return remote(table.at[at(src + n)], table.at[at(dst + n)],
                      f_send.at[kind, n], f_recv.at[kind, n], device)

    a_x, a_z, a_s, b_z, b_s, ha_s, hb_s = [], [], [], [], [], [], []
    for n in range(own_blocks):
        values = feat_ref[n * blk:(n + 1) * blk, :].astype(jnp.float32)
        mean = jnp.sum(values * values, axis=1, keepdims=True) * (1.0 / width)
        scaled = values * lax.rsqrt(mean + epsilon)
        table[at(pos_a + n), :] = (scaled * width ** (-0.5)).astype(jnp.bfloat16)
        a_x.append(fcopy(0, n, pos_a, pos_a, xp))
        a_z.append(fcopy(1, n, pos_a, dst_a, first))
        a_s.append(fcopy(2, n, pos_a, pos_a, sib))
        a_x[n].start()
        a_z[n].start()
        a_s[n].start()
    for n in range(own_blocks):
        a_x[n].wait_recv()
        b_z.append(fcopy(3, n, pos_b, dst_b, second))
        b_s.append(fcopy(4, n, pos_b, pos_b, sib))
        b_z[n].start()
        b_s[n].start()
    for n in range(own_blocks):
        a_s[n].wait_recv()
        b_s[n].wait_recv()

    base_block = g * group_blocks
    row = lax.broadcasted_iota(jnp.int32, (blk, blk), 0)
    col = lax.broadcasted_iota(jnp.int32, (blk, blk), 1)
    for h in range(hubs):
        for n in range(group_blocks):
            off = (hub_ref[h] - (base_block + n)) * 1024
            pick[h * blk:(h + 1) * blk, n * blk:(n + 1) * blk] = jnp.where(
                row - col + off == 0, 1.0, 0.0).astype(jnp.bfloat16)
    low, high = reach * blk, (reach + group_blocks) * blk
    held = jnp.dot(pick[at(q), :], table[low:high, :],
                   preferred_element_type=jnp.float32).astype(jnp.bfloat16)
    for s in range(stages):
        hub_send[s] = held
        copy = remote(hub_send.at[s], hub_recv.at[s], h_send.at[s], h_recv.at[s], partners[s])
        copy.start()
        pending.append(copy)
        copy.wait_recv()
        held = held + hub_recv[s]
    table[at(window + q), :] = held
    hub_copies = []
    for k, device in enumerate((sib, xp, dp)):
        copy = remote(table.at[at(window + q)], table.at[at(window + q)],
                      p_send.at[k], p_recv.at[k], device)
        copy.start()
        hub_copies.append(copy)

    for n in range(own_blocks):
        a_z[n].wait_recv()
        ha_s.append(fcopy(5, n, dst_a, dst_a, sib))
        ha_s[n].start()
    for n in range(own_blocks):
        b_z[n].wait_recv()
        hb_s.append(fcopy(6, n, dst_b, dst_b, sib))
        hb_s[n].start()

    for copy in meta_copies:
        copy.wait_recv()
    for n in range(group_blocks):
        owner, at_n = n // own_blocks, n % own_blocks
        bias[n:n + 1, :] = meta[owner, 8 + at_n:9 + at_n, :]
        line = jnp.broadcast_to(meta[owner, at_n:at_n + 1, :], (blk, blk))
        column = jnp.sum(jnp.where(row == col, line, 0.0), axis=1, keepdims=True)
        label_col[n * blk:(n + 1) * blk, :] = jnp.broadcast_to(column, (blk, blk)).astype(jnp.int32)

    for copy in ha_s + hb_s + hub_copies:
        copy.wait_recv()
    pending += meta_copies + a_x + a_z + a_s + b_z + b_s + ha_s + hb_s + hub_copies

    two = 2 * blk
    row2 = lax.broadcasted_iota(jnp.int32, (two, two), 0)
    col2 = lax.broadcasted_iota(jnp.int32, (two, two), 1)
    factor = LOG2E / kernel_width

    def weigh(m, carry):
        own = table[pl.ds(pl.multiple_of((reach + 2 * m) * blk, blk), two), :]
        lines = (bias[pl.ds(2 * m, 1), :], bias[pl.ds(2 * m + 1, 1), :])
        total = jnp.zeros((two, blk), jnp.float32)
        for k in range(reach + 1 + hubs // 2):
            if k <= reach:
                start = pl.multiple_of(2 * m * blk + k * two, blk)
            else:
                start = window * blk + (k - reach - 1) * two
            slab = table[pl.ds(start, two), :]
            dots = lax.dot_general(own, slab, (((1,), (1,)), ((), ())),
                                   preferred_element_type=jnp.float32)
            dots = dots * factor
            if k <= reach:
                parts = []
                for half in range(2):
                    line = jnp.concatenate(
                        [jnp.broadcast_to(lines[half][:, 2 * k + j:2 * k + j + 1], (1, blk))
                         for j in range(2)], axis=1)
                    parts.append(dots[half * blk:(half + 1) * blk, :] + line)
                value = jnp.exp2(jnp.concatenate(parts, axis=0))
                if 2 * k == reach:
                    value = jnp.where(row2 == col2, 0.0, value)
            else:
                value = jnp.exp2(dots - factor)
                rows_of = []
                for half in range(2):
                    cols_of = []
                    for j in range(2):
                        hub = hub_ref[2 * (k - reach - 1) + j]
                        off = (hub - (base_block + 2 * m + half)) * 1024
                        tile = value[half * blk:(half + 1) * blk, j * blk:(j + 1) * blk]
                        cols_of.append(jnp.where(row - col + off == 0, 0.0, tile))
                    rows_of.append(jnp.concatenate(cols_of, axis=1))
                value = jnp.concatenate(rows_of, axis=0)
            total = total + value[:, :blk] + value[:, blk:]
            weights[m, :, k * two:(k + 1) * two] = value.astype(jnp.bfloat16)
        degree = jnp.sum(total, axis=1, keepdims=True)
        inv_root[pl.ds(pl.multiple_of(m * two, two), two), :] = jnp.broadcast_to(
            lax.rsqrt(degree), (two, blk))
        return carry

    lax.fori_loop(0, pairs, weigh, 0)

    lane = lax.broadcasted_iota(jnp.int32, (two, quarter), 1)

    def wide(ref, m):
        value = ref[pl.ds(pl.multiple_of(m * two, two), two), :]
        return jnp.concatenate([value] * (quarter // blk), axis=1)

    def begin(m, carry):
        seeds = wide(label_col, m) == lane + q * quarter
        labels[0, pl.ds(pl.multiple_of(reach * blk + m * two, blk), two), :] = jnp.where(
            seeds, wide(inv_root, m), 0.0).astype(jnp.bfloat16)
        return carry

    lax.fori_loop(0, pairs, begin, 0)

    half_rows = reach * blk
    for t in range(ITERS):
        z_down = remote(labels.at[t, low:low + half_rows], labels.at[t, high:high + half_rows],
                        z_send.at[t, 0], z_recv.at[t, 0], down)
        z_up = remote(labels.at[t, high - half_rows:high], labels.at[t, 0:half_rows],
                      z_send.at[t, 1], z_recv.at[t, 1], up)
        held = jnp.dot(pick[...], labels[t, low:high, :],
                       preferred_element_type=jnp.float32).astype(jnp.bfloat16)
        for s in range(stages):
            lab_send[t, s] = held
            copy = remote(lab_send.at[t, s], lab_recv.at[t, s],
                          l_send.at[t, s], l_recv.at[t, s], partners[s])
            copy.start()
            if s == 0:
                z_down.start()
                z_up.start()
            pending.append(copy)
            copy.wait_recv()
            held = held + lab_recv[t, s]
        labels[t, window * blk:(window + hubs) * blk, :] = held
        z_down.wait_recv()
        z_up.wait_recv()
        pending += [z_down, z_up]

        def apply(m, carry):
            total = jnp.dot(weights[m, :, :span],
                            labels[t, pl.ds(pl.multiple_of(m * two, two), span), :],
                            preferred_element_type=jnp.float32)
            total = total + jnp.dot(weights[m, :, span:],
                                    labels[t, window * blk:(window + hubs) * blk, :],
                                    preferred_element_type=jnp.float32)
            root = wide(inv_root, m)
            spread = spread_rate * root * total
            if t < ITERS - 1:
                seeds = wide(label_col, m) == lane + q * quarter
                spread = spread + jnp.where(seeds, 1.0 - spread_rate, 0.0)
                labels[t + 1, pl.ds(pl.multiple_of(reach * blk + m * two, blk), two), :] = (
                    root * spread).astype(jnp.bfloat16)
            else:
                rows = pl.ds(pl.multiple_of(m * two, two), two)
                res[rows, :] = spread
                res_half[rows, :] = spread.astype(jnp.bfloat16)
            return carry

        lax.fori_loop(0, pairs, apply, 0)

    own_rows = own_blocks * blk

    def rows_of(index):
        return pl.ds(pl.multiple_of(index * own_rows, blk), own_rows)

    last = [
        remote(res_half.at[rows_of(q_x)], from_x, r_send.at[1], r_recv.at[1], xp),
        remote(res_half.at[rows_of(q_d)], from_d, r_send.at[2], r_recv.at[2], dp),
        remote(res.at[rows_of(q_sib)], from_sib, r_send.at[0], r_recv.at[0], sib),
    ]
    for copy in last:
        copy.start()
    for copy in last:
        copy.wait_recv()
    pending += last

    lane1 = lax.broadcasted_iota(jnp.int32, (blk, quarter), 1)
    for n in range(own_blocks):
        rows = pl.ds(n * blk, blk)
        group_rows = pl.ds(pl.multiple_of(q * own_rows + n * blk, blk), blk)
        label = label_col[group_rows, :]
        label = jnp.concatenate([label] * (quarter // blk), axis=1)
        pieces = [(q, res[group_rows, :]), (q_sib, from_sib[rows, :]),
                  (q_x, from_x[rows, :].astype(jnp.float32)),
                  (q_d, from_d[rows, :].astype(jnp.float32))]
        values = []
        total = jnp.zeros((blk, 1), jnp.float32)
        for index, piece in pieces:
            seeds = label == lane1 + index * quarter
            value = piece + jnp.where(seeds, 1.0 - spread_rate, 0.0)
            total = total + jnp.sum(value, axis=1, keepdims=True)
            values.append((index, value))
        scale = cols / total
        for index, value in values:
            out_ref[rows, pl.ds(pl.multiple_of(index * quarter, quarter), quarter)] = jnp.log(
                1.0 + value * scale)
    for copy in pending:
        copy.wait_send()


def on_device(cols, features, seed_labels, neighbours, hub_blocks):
    device = lax.axis_index("rows")
    devices = lax.axis_size("rows")
    own_blocks, slots = neighbours.shape
    rows, width = features.shape
    blk = rows // own_blocks
    all_blocks = devices * own_blocks
    reach = 2 * own_blocks
    groups = devices // GROUP
    stages = groups.bit_length() - 1
    group_blocks = GROUP * own_blocks
    table_rows = (group_blocks + 2 * reach + GROUP) * blk
    pairs = group_blocks // 2
    span = (2 * reach + 2 + GROUP) * blk
    quarter = cols // GROUP

    ids = device * own_blocks + jnp.arange(own_blocks, dtype=jnp.int32)
    parity = ids % 2
    position = (neighbours - ids[:, None] + reach + all_blocks) % all_blocks + parity[:, None]
    count = jnp.sum(
        (position[:, :, None] == jnp.arange(128, dtype=jnp.int32)[None, None, :]), axis=1
    ).astype(jnp.float32)
    bias = jnp.where(count > 0, jnp.log2(jnp.maximum(count, 1.0)) - LOG2E / kernel_width, -1e4)
    lines = seed_labels.reshape(own_blocks, blk).astype(jnp.float32)
    pad = ((0, 8 - own_blocks), (0, 0))
    meta = jnp.concatenate([jnp.pad(lines, pad), jnp.pad(bias, pad)], axis=0)

    vmem = pl.BlockSpec(memory_space=pltpu.VMEM)
    dma = pltpu.SemaphoreType.DMA
    return pl.pallas_call(
        functools.partial(kernel, groups, blk, cols),
        out_shape=jax.ShapeDtypeStruct((rows, cols), jnp.float32),
        in_specs=[vmem, vmem, pl.BlockSpec(memory_space=pltpu.SMEM)],
        out_specs=vmem,
        scratch_shapes=[
            pltpu.VMEM((table_rows, width), jnp.bfloat16),
            pltpu.VMEM((pairs, 2 * blk, span), jnp.bfloat16),
            pltpu.VMEM((ITERS, table_rows, quarter), jnp.bfloat16),
            pltpu.VMEM((group_blocks * blk, blk), jnp.float32),
            pltpu.VMEM((group_blocks * blk, blk), jnp.int32),
            pltpu.VMEM((GROUP, 16, 128), jnp.float32),
            pltpu.VMEM((group_blocks + 4, 128), jnp.float32),
            pltpu.VMEM((stages, blk, width), jnp.bfloat16),
            pltpu.VMEM((stages, blk, width), jnp.bfloat16),
            pltpu.VMEM((ITERS, stages, GROUP * blk, quarter), jnp.bfloat16),
            pltpu.VMEM((ITERS, stages, GROUP * blk, quarter), jnp.bfloat16),
            pltpu.VMEM((group_blocks * blk, quarter), jnp.float32),
            pltpu.VMEM((group_blocks * blk, quarter), jnp.bfloat16),
            pltpu.VMEM((rows, quarter), jnp.float32),
            pltpu.VMEM((rows, quarter), jnp.bfloat16),
            pltpu.VMEM((rows, quarter), jnp.bfloat16),
            pltpu.VMEM((GROUP * blk, group_blocks * blk), jnp.bfloat16),
            dma((7, own_blocks)), dma((7, own_blocks)),
            dma((3,)), dma((3,)),
            dma((stages,)), dma((stages,)),
            dma((3,)), dma((3,)),
            dma((ITERS, 2)), dma((ITERS, 2)),
            dma((ITERS, stages)), dma((ITERS, stages)),
            dma((3,)), dma((3,)),
        ],
        compiler_params=pltpu.CompilerParams(
            collective_id=0, has_side_effects=True, vmem_limit_bytes=60 * 1024 * 1024),
    )(features, meta, hub_blocks)


def solution(mesh):
    placed = (
        P(("region", "rows"), None),
        P(("region", "rows")),
        P(("region", "rows"), None),
        P("region"),
    )
    return jax.shard_map(
        functools.partial(on_device, 1024),
        mesh=mesh,
        in_specs=placed,
        out_specs=P(("region", "rows"), None),
        check_vma=False,
    )
```

time: 2000 us -> 259 us (0.13); the launches traced: 1980 us -> 259 us
  loops' own time: 837 us -> 0 us
  matrix products: 496 us -> 0 us
  waiting for transfers between devices: 447 us -> 0 us
  Pallas kernels: 0 us -> 253 us
  local copies, waits for them, and re-layouts: 115 us -> 3.56 us
  other arithmetic: 32.7 us -> 2.17 us
  starting transfers between devices: 27.8 us -> 0 us
  between operations: 23.2 us -> 0.02 us
    another operation x4 -> x0, loops' own time: 837 us -> none  [the longest x3 530 us: on_device(): lax.map(apply, (weights, table_index)).reshape(block_count * block_rows, C)]
    dot_general x400 -> x0, matrix products: 496 us -> none  [the longest x300 370 us: apply(): jnp.dot(part_weights, slab, preferred_element_type=jnp.float32)]
    ppermute x16 -> x0, waiting for transfers between devices: 279 us -> none  [from_behind(): return lax.ppermute(value, axis, pairs)]
    pallas_call x0 -> x1, Pallas kernels: none -> 253 us  [on_device(): pl.pallas_call(functools.partial(kernel, groups, blk, cols), out_shape=ja...]
    psum x4 -> x0, waiting for transfers between devices: 168 us -> none  [spread_2(): return lax.psum(block, axis)]
    unnamed x37 -> x1, local copies, waits for them, and re-layouts: 56.7 us -> 3.56 us
    ppermute x16 -> x0, starting transfers between devices: 27.7 us -> none  [from_behind(): return lax.ppermute(value, axis, pairs)]
  transfers between devices with their start and end apart: 20 -> 0, of which waited for: 12 -> 0; matrix products, arithmetic and copies ran while one was open for 3% -> 0% of each run, Pallas kernels for 0% -> 0%
where the time goes in v1:
time: 259 us
  Pallas kernels  253 us (98%)
  local copies, waits for them, and re-layouts  3.56 us (1%)
    pallas_call x1, Pallas kernels, on_device(): pl.pallas_call(functools.partial(kernel, groups, blk, cols), out_shape=ja...  253 us

profile of v1, /device:TPU:1, one launch (start us, length us, event | category | flops | bytes accessed | tf_op | source)
XLA Modules:
  0.0 258.7 jit_solution(17799869194996411193)
XLA Ops:
  0.0 0.8 fusion
  0.8 0.1 convert_reduce_fusion
  0.9 0.7 convert_bitcast_fusion
  1.6 0.6 select_maximum_fusion.meta_ref
  2.2 253.0 %shard_map.46 = f32[640,1024]{1,0:T(8,128)} custom-call(bf16[640,768]{1,0:T(8,128)(2,1)} %feat_ref.1, f32[16,128]{1,0:T(8,128)} %select_maximum_fusion.meta_ref, s32[4]{0:T(128)} %hub_ref.1), custom_call_target="tpu_custom_call" | custom-call | tf_op jit(solution)/shard_map/pallas_call | solution.py:335
  255.2 3.6 %copy.6 = f32[640,1024]{1,0:T(8,128)} copy(f32[640,1024]{1,0:T(8,128)} %shard_map.46) | data formatting | bytes 5242880
  (2 shorter events, 0.0 us)

commit v2 on v1

--- a/solution.py
+++ b/solution.py
@@ -19,9 +19,9 @@
 
 def kernel(groups, blk, cols, feat_ref, meta_ref, hub_ref, out_ref,
            table, weights, labels, inv_root, label_col, meta, bias,
-           hub_send, hub_recv, lab_send, lab_recv, res, res_half, from_sib, from_x, from_d, pick,
-           f_send, f_recv, m_send, m_recv, h_send, h_recv, p_send, p_recv,
-           z_send, z_recv, l_send, l_recv, r_send, r_recv):
+           hub_bufs, small_bufs, lab_bufs, lines, res, res_half, from_sib, from_x, from_d, pick,
+           f_send, f_recv, m_send, m_recv, p_send, p_recv, n_send, n_recv,
+           c_send, c_recv, z_send, z_recv, r_send, r_recv):
     own_blocks = feat_ref.shape[0] // blk
     width = feat_ref.shape[1]
     reach = 2 * own_blocks
@@ -31,7 +31,6 @@
     pairs = group_blocks // 2
     span = (2 * reach + 2) * blk
     quarter = cols // GROUP
-    stages = groups.bit_length() - 1
 
     me = lax.axis_index("rows")
     g, q = lax.div(me, GROUP), lax.rem(me, GROUP)
@@ -44,25 +43,60 @@
     down = lax.rem(g + groups - 1, groups) * GROUP + q
     first = x * up + (1 - x) * down
     second = x * down + (1 - x) * up
-    partners = []
-    for s in range(stages):
-        size = 2 ** (s + 1)
-        pg = lax.div(g, size) * size + size - 1 - lax.rem(g, size)
-        partners.append(pg * GROUP + q)
-
     def remote(src, dst, send, recv, device):
         return pltpu.make_async_remote_copy(
             src_ref=src, dst_ref=dst, send_sem=send, recv_sem=recv,
             device_id={"rows": device}, device_id_type=pl.DeviceIdType.MESH)
 
     barrier = pltpu.get_barrier_semaphore()
-    everyone = [sib, xp, dp, up, down] + partners
+    everyone = [sib, xp, dp, up, down]
     for device in everyone:
         pl.semaphore_signal(barrier, inc=1, device_id={"rows": device},
                             device_id_type=pl.DeviceIdType.MESH)
     pl.semaphore_wait(barrier, len(everyone))
 
     pending = []
+    ends = []
+
+    def chain(held, bufs, index, between):
+        to_up = remote(bufs.at[2], bufs.at[0], c_send.at[index, 0], c_recv.at[index, 0], up)
+        to_down = remote(bufs.at[3], bufs.at[1], c_send.at[index, 1], c_recv.at[index, 1], down)
+        ends.append((to_up, to_down))
+        inner = jnp.logical_and(g > 0, g < groups - 1)
+
+        @pl.when(g == 0)
+        def _():
+            bufs[0] = jnp.zeros_like(held)
+            bufs[2] = held
+            to_up.start()
+
+        @pl.when(g == groups - 1)
+        def _():
+            bufs[1] = jnp.zeros_like(held)
+            bufs[3] = held
+            to_down.start()
+
+        between()
+
+        @pl.when(g > 0)
+        def _():
+            to_up.wait_recv()
+
+        @pl.when(inner)
+        def _():
+            bufs[2] = held + bufs[0]
+            to_up.start()
+
+        @pl.when(g < groups - 1)
+        def _():
+            to_down.wait_recv()
+
+        @pl.when(inner)
+        def _():
+            bufs[3] = held + bufs[1]
+            to_down.start()
+
+        return held + bufs[0] + bufs[1]
 
     def at(position):
         return pl.ds(pl.multiple_of(position * blk, blk), blk)
@@ -117,13 +151,70 @@
     low, high = reach * blk, (reach + group_blocks) * blk
     held = jnp.dot(pick[at(q), :], table[low:high, :],
                    preferred_element_type=jnp.float32).astype(jnp.bfloat16)
-    for s in range(stages):
-        hub_send[s] = held
-        copy = remote(hub_send.at[s], hub_recv.at[s], h_send.at[s], h_recv.at[s], partners[s])
-        copy.start()
-        pending.append(copy)
+    for copy in meta_copies:
         copy.wait_recv()
-        held = held + hub_recv[s]
+    lines[0] = jnp.zeros_like(lines[0])
+    for n in range(group_blocks):
+        owner, at_n = n // own_blocks, n % own_blocks
+        for p in range(reach * 2 + 2):
+            bias[n:n + 1, p * blk:(p + 1) * blk] = jnp.broadcast_to(
+                meta[owner, 8 + at_n:9 + at_n, p:p + 1], (1, blk))
+        line = meta[owner, at_n:at_n + 1, :]
+        lines[0, 24 + n:25 + n, :] = line
+        line = jnp.broadcast_to(line, (blk, blk))
+        column = jnp.sum(jnp.where(row == col, line, 0.0), axis=1, keepdims=True)
+        label_col[n * blk:(n + 1) * blk, :] = jnp.broadcast_to(column, (blk, blk)).astype(jnp.int32)
+
+    two = 2 * blk
+    row2 = lax.broadcasted_iota(jnp.int32, (two, two), 0)
+    col2 = lax.broadcasted_iota(jnp.int32, (two, two), 1)
+    factor = LOG2E / kernel_width
+    chunks = reach + 1
+
+    def step(value, unit):
+        return value * unit if isinstance(value, int) else pl.multiple_of(value * unit, unit)
+
+    def add_degree(m, value):
+        rows = pl.ds(step(m, two), two)
+        inv_root[rows, :] += value[:, :blk] + value[:, blk:]
+
+    def chunk(m, k):
+        own = table[pl.ds(step(m, two) + reach * blk, two), :]
+        slab = table[pl.ds(step(m + k, two), two), :]
+        dots = lax.dot_general(own, slab, (((1,), (1,)), ((), ())),
+                               preferred_element_type=jnp.float32)
+        there = pl.ds(step(k, two), two)
+        value = jnp.exp2(jnp.concatenate(
+            [dots[:blk, :] * factor + bias[pl.ds(2 * m, 1), there],
+             dots[blk:, :] * factor + bias[pl.ds(2 * m + 1, 1), there]], axis=0))
+        if not isinstance(k, int):
+            value = jnp.where(row2 - col2 + (2 * k - reach) * 1024 == 0, 0.0, value)
+        elif 2 * k == reach:
+            value = jnp.where(row2 == col2, 0.0, value)
+        add_degree(m, value)
+        weights[m, :, there] = value.astype(jnp.bfloat16)
+
+    inv_root[...] = jnp.zeros_like(inv_root)
+    half = reach // 2
+
+    def inside(m):
+        lowest = max(half - m, 0) if isinstance(m, int) else jnp.maximum(half - m, 0)
+        highest = (min(half + pairs - 1 - m, reach) if isinstance(m, int)
+                   else jnp.minimum(half + pairs - 1 - m, reach))
+        return lowest, (highest - lowest + 1) // 2 if isinstance(m, int) else lax.div(
+            highest - lowest + 1, 2)
+
+    def weigh_inside(m, carry):
+        lowest, count = inside(m)
+
+        def body(i, carry):
+            chunk(m, lowest + 2 * i)
+            chunk(m, lowest + 2 * i + 1)
+            return carry
+
+        return lax.fori_loop(0, count, body, carry)
+
+    held = chain(held, hub_bufs, 0, lambda: lax.fori_loop(0, pairs // 2, weigh_inside, 0))
     table[at(window + q), :] = held
     hub_copies = []
     for k, device in enumerate((sib, xp, dp)):
@@ -131,6 +222,7 @@
                       p_send.at[k], p_recv.at[k], device)
         copy.start()
         hub_copies.append(copy)
+    lax.fori_loop(pairs // 2, pairs, weigh_inside, 0)
 
     for n in range(own_blocks):
         a_z[n].wait_recv()
@@ -141,105 +233,113 @@
         hb_s.append(fcopy(6, n, dst_b, dst_b, sib))
         hb_s[n].start()
 
-    for copy in meta_copies:
-        copy.wait_recv()
-    for n in range(group_blocks):
-        owner, at_n = n // own_blocks, n % own_blocks
-        bias[n:n + 1, :] = meta[owner, 8 + at_n:9 + at_n, :]
-        line = jnp.broadcast_to(meta[owner, at_n:at_n + 1, :], (blk, blk))
-        column = jnp.sum(jnp.where(row == col, line, 0.0), axis=1, keepdims=True)
-        label_col[n * blk:(n + 1) * blk, :] = jnp.broadcast_to(column, (blk, blk)).astype(jnp.int32)
-
     for copy in ha_s + hb_s + hub_copies:
         copy.wait_recv()
     pending += meta_copies + a_x + a_z + a_s + b_z + b_s + ha_s + hb_s + hub_copies
 
-    two = 2 * blk
-    row2 = lax.broadcasted_iota(jnp.int32, (two, two), 0)
-    col2 = lax.broadcasted_iota(jnp.int32, (two, two), 1)
-    factor = LOG2E / kernel_width
-
-    def weigh(m, carry):
-        own = table[pl.ds(pl.multiple_of((reach + 2 * m) * blk, blk), two), :]
-        lines = (bias[pl.ds(2 * m, 1), :], bias[pl.ds(2 * m + 1, 1), :])
+    for m in range(pairs):
+        lowest, count = inside(m)
+        for k in range(chunks):
+            if not lowest <= k < lowest + 2 * count:
+                chunk(m, k)
+
+    def weigh_hubs(m, carry):
+        own = table[pl.ds(step(m, two) + reach * blk, two), :]
         total = jnp.zeros((two, blk), jnp.float32)
-        for k in range(reach + 1 + hubs // 2):
-            if k <= reach:
-                start = pl.multiple_of(2 * m * blk + k * two, blk)
-            else:
-                start = window * blk + (k - reach - 1) * two
-            slab = table[pl.ds(start, two), :]
+        for k in range(hubs // 2):
+            slab = table[pl.ds(window * blk + k * two, two), :]
             dots = lax.dot_general(own, slab, (((1,), (1,)), ((), ())),
                                    preferred_element_type=jnp.float32)
-            dots = dots * factor
-            if k <= reach:
-                parts = []
-                for half in range(2):
-                    line = jnp.concatenate(
-                        [jnp.broadcast_to(lines[half][:, 2 * k + j:2 * k + j + 1], (1, blk))
-                         for j in range(2)], axis=1)
-                    parts.append(dots[half * blk:(half + 1) * blk, :] + line)
-                value = jnp.exp2(jnp.concatenate(parts, axis=0))
-                if 2 * k == reach:
-                    value = jnp.where(row2 == col2, 0.0, value)
-            else:
-                value = jnp.exp2(dots - factor)
-                rows_of = []
-                for half in range(2):
-                    cols_of = []
-                    for j in range(2):
-                        hub = hub_ref[2 * (k - reach - 1) + j]
-                        off = (hub - (base_block + 2 * m + half)) * 1024
-                        tile = value[half * blk:(half + 1) * blk, j * blk:(j + 1) * blk]
-                        cols_of.append(jnp.where(row - col + off == 0, 0.0, tile))
-                    rows_of.append(jnp.concatenate(cols_of, axis=1))
-                value = jnp.concatenate(rows_of, axis=0)
+            value = jnp.exp2(dots * factor - factor)
+            rows_of = []
+            for part in range(2):
+                cols_of = []
+                for j in range(2):
+                    off = (hub_ref[2 * k + j] - (base_block + 2 * m + part)) * 1024
+                    tile = value[part * blk:(part + 1) * blk, j * blk:(j + 1) * blk]
+                    cols_of.append(jnp.where(row - col + off == 0, 0.0, tile))
+                rows_of.append(jnp.concatenate(cols_of, axis=1))
+            value = jnp.concatenate(rows_of, axis=0)
             total = total + value[:, :blk] + value[:, blk:]
-            weights[m, :, k * two:(k + 1) * two] = value.astype(jnp.bfloat16)
-        degree = jnp.sum(total, axis=1, keepdims=True)
-        inv_root[pl.ds(pl.multiple_of(m * two, two), two), :] = jnp.broadcast_to(
-            lax.rsqrt(degree), (two, blk))
+            weights[m, :, span + k * two:span + (k + 1) * two] = value.astype(jnp.bfloat16)
+        rows = pl.ds(step(m, two), two)
+        degree = jnp.sum(inv_root[rows, :] + total, axis=1, keepdims=True)
+        inv_root[rows, :] = jnp.broadcast_to(lax.rsqrt(degree), (two, blk))
         return carry
 
-    lax.fori_loop(0, pairs, weigh, 0)
+    lax.fori_loop(0, pairs, weigh_hubs, 0)
 
     lane = lax.broadcasted_iota(jnp.int32, (two, quarter), 1)
+    lane1 = lax.broadcasted_iota(jnp.int32, (blk, quarter), 1)
 
     def wide(ref, m):
-        value = ref[pl.ds(pl.multiple_of(m * two, two), two), :]
+        value = ref[pl.ds(step(m, two), two), :]
         return jnp.concatenate([value] * (quarter // blk), axis=1)
+
+    for n in range(group_blocks):
+        lines[0, n:n + 1, :] = jnp.sum(
+            jnp.where(row == col, inv_root[n * blk:(n + 1) * blk, :], 0.0), axis=0, keepdims=True)
+    n_up = remote(lines.at[0], lines.at[1], n_send.at[0], n_recv.at[0], up)
+    n_down = remote(lines.at[0], lines.at[2], n_send.at[1], n_recv.at[1], down)
+    pending += [n_up, n_down]
+    block_row = lax.broadcasted_iota(jnp.int32, (group_blocks, blk), 0) + base_block
+    found = []
+    for start in (0, 24):
+        for h in range(hubs):
+            found.append(jnp.sum(jnp.where(block_row - hub_ref[h] == 0,
+                                           lines[0, start:start + group_blocks, :], 0.0),
+                                 axis=0, keepdims=True))
+    low_block = reach + group_blocks
 
     def begin(m, carry):
         seeds = wide(label_col, m) == lane + q * quarter
-        labels[0, pl.ds(pl.multiple_of(reach * blk + m * two, blk), two), :] = jnp.where(
+        labels[0, pl.ds(step(m, two) + reach * blk, two), :] = jnp.where(
             seeds, wide(inv_root, m), 0.0).astype(jnp.bfloat16)
         return carry
 
-    lax.fori_loop(0, pairs, begin, 0)
+    def between_small():
+        n_up.start()
+        n_down.start()
+        lax.fori_loop(0, pairs, begin, 0)
+
+    small = chain(jnp.concatenate(found, axis=0), small_bufs, 1, between_small)
+    n_up.wait_recv()
+    n_down.wait_recv()
+
+    def first_labels(position, root, label):
+        def column(line):
+            return jnp.sum(jnp.where(row == col, jnp.broadcast_to(line, (blk, blk)), 0.0),
+                           axis=1, keepdims=True)
+        seeds = column(label).astype(jnp.int32) == lane1 + q * quarter
+        labels[0, position * blk:(position + 1) * blk, :] = jnp.where(
+            seeds, column(root), 0.0).astype(jnp.bfloat16)
+
+    for n in range(reach):
+        at_n = group_blocks - reach + n
+        first_labels(n, lines[1, at_n:at_n + 1, :], lines[1, 24 + at_n:25 + at_n, :])
+        first_labels(low_block + n, lines[2, n:n + 1, :], lines[2, 24 + n:25 + n, :])
+    for h in range(hubs):
+        first_labels(window + h, small[h:h + 1, :], small[hubs + h:hubs + h + 1, :])
 
     half_rows = reach * blk
     for t in range(ITERS):
-        z_down = remote(labels.at[t, low:low + half_rows], labels.at[t, high:high + half_rows],
-                        z_send.at[t, 0], z_recv.at[t, 0], down)
-        z_up = remote(labels.at[t, high - half_rows:high], labels.at[t, 0:half_rows],
-                      z_send.at[t, 1], z_recv.at[t, 1], up)
-        held = jnp.dot(pick[...], labels[t, low:high, :],
-                       preferred_element_type=jnp.float32).astype(jnp.bfloat16)
-        for s in range(stages):
-            lab_send[t, s] = held
-            copy = remote(lab_send.at[t, s], lab_recv.at[t, s],
-                          l_send.at[t, s], l_recv.at[t, s], partners[s])
-            copy.start()
-            if s == 0:
+        if t > 0:
+            z_down = remote(labels.at[t, low:low + half_rows], labels.at[t, high:high + half_rows],
+                            z_send.at[t - 1, 0], z_recv.at[t - 1, 0], down)
+            z_up = remote(labels.at[t, high - half_rows:high], labels.at[t, 0:half_rows],
+                          z_send.at[t - 1, 1], z_recv.at[t - 1, 1], up)
+            held = jnp.dot(pick[...], labels[t, low:high, :],
+                           preferred_element_type=jnp.float32).astype(jnp.bfloat16)
+
+            def start_halo():
                 z_down.start()
                 z_up.start()
-            pending.append(copy)
-            copy.wait_recv()
-            held = held + lab_recv[t, s]
-        labels[t, window * blk:(window + hubs) * blk, :] = held
-        z_down.wait_recv()
-        z_up.wait_recv()
-        pending += [z_down, z_up]
+
+            labels[t, window * blk:(window + hubs) * blk, :] = chain(
+                held, lab_bufs.at[t - 1], 1 + t, start_halo)
+            z_down.wait_recv()
+            z_up.wait_recv()
+            pending += [z_down, z_up]
 
         def apply(m, carry):
             total = jnp.dot(weights[m, :, :span],
@@ -261,7 +361,8 @@
                 res_half[rows, :] = spread.astype(jnp.bfloat16)
             return carry
 
-        lax.fori_loop(0, pairs, apply, 0)
+        if t < ITERS - 1:
+            lax.fori_loop(0, pairs, apply, 0)
 
     own_rows = own_blocks * blk
 
@@ -273,13 +374,17 @@
         remote(res_half.at[rows_of(q_d)], from_d, r_send.at[2], r_recv.at[2], dp),
         remote(res.at[rows_of(q_sib)], from_sib, r_send.at[0], r_recv.at[0], sib),
     ]
-    for copy in last:
-        copy.start()
+    there = (1 - x) * (pairs // 2)
+    lax.fori_loop(0, pairs // 2, lambda m, carry: apply(there + m, carry), 0)
+    last[0].start()
+    last[1].start()
+    here = x * (pairs // 2)
+    lax.fori_loop(0, pairs // 2, lambda m, carry: apply(here + m, carry), 0)
+    last[2].start()
     for copy in last:
         copy.wait_recv()
     pending += last
 
-    lane1 = lax.broadcasted_iota(jnp.int32, (blk, quarter), 1)
     for n in range(own_blocks):
         rows = pl.ds(n * blk, blk)
         group_rows = pl.ds(pl.multiple_of(q * own_rows + n * blk, blk), blk)
@@ -301,6 +406,14 @@
                 1.0 + value * scale)
     for copy in pending:
         copy.wait_send()
+    for to_up, to_down in ends:
+        @pl.when(g < groups - 1)
+        def _():
+            to_up.wait_send()
+
+        @pl.when(g > 0)
+        def _():
+            to_down.wait_send()
 
 
 def on_device(cols, features, seed_labels, neighbours, hub_blocks):
@@ -312,7 +425,6 @@
     all_blocks = devices * own_blocks
     reach = 2 * own_blocks
     groups = devices // GROUP
-    stages = groups.bit_length() - 1
     group_blocks = GROUP * own_blocks
     table_rows = (group_blocks + 2 * reach + GROUP) * blk
     pairs = group_blocks // 2
@@ -344,11 +456,11 @@
             pltpu.VMEM((group_blocks * blk, blk), jnp.float32),
             pltpu.VMEM((group_blocks * blk, blk), jnp.int32),
             pltpu.VMEM((GROUP, 16, 128), jnp.float32),
-            pltpu.VMEM((group_blocks + 4, 128), jnp.float32),
-            pltpu.VMEM((stages, blk, width), jnp.bfloat16),
-            pltpu.VMEM((stages, blk, width), jnp.bfloat16),
-            pltpu.VMEM((ITERS, stages, GROUP * blk, quarter), jnp.bfloat16),
-            pltpu.VMEM((ITERS, stages, GROUP * blk, quarter), jnp.bfloat16),
+            pltpu.VMEM((group_blocks, (2 * reach + 2) * blk), jnp.float32),
+            pltpu.VMEM((4, blk, width), jnp.bfloat16),
+            pltpu.VMEM((4, 2 * GROUP, 128), jnp.float32),
+            pltpu.VMEM((ITERS - 1, 4, GROUP * blk, quarter), jnp.bfloat16),
+            pltpu.VMEM((3, 48, 128), jnp.float32),
             pltpu.VMEM((group_blocks * blk, quarter), jnp.float32),
             pltpu.VMEM((group_blocks * blk, quarter), jnp.bfloat16),
             pltpu.VMEM((rows, quarter), jnp.float32),
@@ -357,10 +469,10 @@
             pltpu.VMEM((GROUP * blk, group_blocks * blk), jnp.bfloat16),
             dma((7, own_blocks)), dma((7, own_blocks)),
             dma((3,)), dma((3,)),
-            dma((stages,)), dma((stages,)),
             dma((3,)), dma((3,)),
-            dma((ITERS, 2)), dma((ITERS, 2)),
-            dma((ITERS, stages)), dma((ITERS, stages)),
+            dma((2,)), dma((2,)),
+            dma((ITERS + 1, 2)), dma((ITERS + 1, 2)),
+            dma((ITERS - 1, 2)), dma((ITERS - 1, 2)),
             dma((3,)), dma((3,)),
         ],
         compiler_params=pltpu.CompilerParams(

time: 259 us -> 228 us (0.88)
  Pallas kernels: 253 us -> 222 us
    pallas_call x1, Pallas kernels: 253 us -> 222 us  [on_device(): pl.pallas_call(functools.partial(kernel, groups, blk, cols), out_shape=ja...]
where the time goes in v2:
time: 228 us
  Pallas kernels  222 us (97%)
  local copies, waits for them, and re-layouts  3.56 us (2%)
    pallas_call x1, Pallas kernels, on_device(): pl.pallas_call(functools.partial(kernel, groups, blk, cols), out_shape=ja...  222 us

profile of v2, /device:TPU:1, one launch (start us, length us, event | category | flops | bytes accessed | tf_op | source)
XLA Modules:
  0.0 227.9 jit_solution(3287002934241174245)
XLA Ops:
  0.0 0.8 fusion
  0.8 0.1 convert_reduce_fusion
  0.9 0.7 convert_bitcast_fusion
  1.6 0.6 select_maximum_fusion.meta_ref
  2.2 222.2 %shard_map.46 = f32[640,1024]{1,0:T(8,128)} custom-call(bf16[640,768]{1,0:T(8,128)(2,1)} %feat_ref.1, f32[16,128]{1,0:T(8,128)} %select_maximum_fusion.meta_ref, s32[4]{0:T(128)} %hub_ref.1), custom_call_target="tpu_custom_call" | custom-call | tf_op jit(solution)/shard_map/pallas_call | solution.py:447
  224.4 3.6 %copy.6 = f32[640,1024]{1,0:T(8,128)} copy(f32[640,1024]{1,0:T(8,128)} %shard_map.46) | data formatting | bytes 5242880
  (2 shorter events, 0.0 us)

commit v3 on v2

--- a/solution.py
+++ b/solution.py
@@ -58,9 +58,13 @@
     pending = []
     ends = []
 
-    def chain(held, bufs, index, between):
-        to_up = remote(bufs.at[2], bufs.at[0], c_send.at[index, 0], c_recv.at[index, 0], up)
-        to_down = remote(bufs.at[3], bufs.at[1], c_send.at[index, 1], c_recv.at[index, 1], down)
+    def chain(held, bufs, index, between, parts):
+        count = held.shape[0] // parts
+        rows = [slice(n * count, (n + 1) * count) for n in range(parts)]
+        to_up = [remote(bufs.at[2, r], bufs.at[0, r], c_send.at[index, 0, n],
+                        c_recv.at[index, 0, n], up) for n, r in enumerate(rows)]
+        to_down = [remote(bufs.at[3, r], bufs.at[1, r], c_send.at[index, 1, n],
+                          c_recv.at[index, 1, n], down) for n, r in enumerate(rows)]
         ends.append((to_up, to_down))
         inner = jnp.logical_and(g > 0, g < groups - 1)
 
@@ -68,33 +72,36 @@
         def _():
             bufs[0] = jnp.zeros_like(held)
             bufs[2] = held
-            to_up.start()
+            for copy in to_up:
+                copy.start()
 
         @pl.when(g == groups - 1)
         def _():
             bufs[1] = jnp.zeros_like(held)
             bufs[3] = held
-            to_down.start()
+            for copy in to_down:
+                copy.start()
 
         between()
 
-        @pl.when(g > 0)
-        def _():
-            to_up.wait_recv()
-
-        @pl.when(inner)
-        def _():
-            bufs[2] = held + bufs[0]
-            to_up.start()
-
-        @pl.when(g < groups - 1)
-        def _():
-            to_down.wait_recv()
-
-        @pl.when(inner)
-        def _():
-            bufs[3] = held + bufs[1]
-            to_down.start()
+        for n, r in enumerate(rows):
+            @pl.when(g > 0)
+            def _():
+                to_up[n].wait_recv()
+
+            @pl.when(inner)
+            def _():
+                bufs[2, r, :] = held[r, :] + bufs[0, r, :]
+                to_up[n].start()
+
+            @pl.when(g < groups - 1)
+            def _():
+                to_down[n].wait_recv()
+
+            @pl.when(inner)
+            def _():
+                bufs[3, r, :] = held[r, :] + bufs[1, r, :]
+                to_down[n].start()
 
         return held + bufs[0] + bufs[1]
 
@@ -214,7 +221,7 @@
 
         return lax.fori_loop(0, count, body, carry)
 
-    held = chain(held, hub_bufs, 0, lambda: lax.fori_loop(0, pairs // 2, weigh_inside, 0))
+    held = chain(held, hub_bufs, 0, lambda: lax.fori_loop(0, pairs // 2, weigh_inside, 0), 4)
     table[at(window + q), :] = held
     hub_copies = []
     for k, device in enumerate((sib, xp, dp)):
@@ -302,7 +309,7 @@
         n_down.start()
         lax.fori_loop(0, pairs, begin, 0)
 
-    small = chain(jnp.concatenate(found, axis=0), small_bufs, 1, between_small)
+    small = chain(jnp.concatenate(found, axis=0), small_bufs, 1, between_small, 1)
     n_up.wait_recv()
     n_down.wait_recv()
 
@@ -324,22 +331,27 @@
     half_rows = reach * blk
     for t in range(ITERS):
         if t > 0:
-            z_down = remote(labels.at[t, low:low + half_rows], labels.at[t, high:high + half_rows],
-                            z_send.at[t - 1, 0], z_recv.at[t - 1, 0], down)
-            z_up = remote(labels.at[t, high - half_rows:high], labels.at[t, 0:half_rows],
-                          z_send.at[t - 1, 1], z_recv.at[t - 1, 1], up)
+            halo = []
+            for n in range(reach):
+                at_n = n * blk
+                halo.append(remote(labels.at[t, low + at_n:low + at_n + blk],
+                                   labels.at[t, high + at_n:high + at_n + blk],
+                                   z_send.at[t - 1, 0, n], z_recv.at[t - 1, 0, n], down))
+                halo.append(remote(labels.at[t, high - half_rows + at_n:high - half_rows + at_n + blk],
+                                   labels.at[t, at_n:at_n + blk],
+                                   z_send.at[t - 1, 1, n], z_recv.at[t - 1, 1, n], up))
             held = jnp.dot(pick[...], labels[t, low:high, :],
                            preferred_element_type=jnp.float32).astype(jnp.bfloat16)
 
             def start_halo():
-                z_down.start()
-                z_up.start()
+                for copy in halo:
+                    copy.start()
 
             labels[t, window * blk:(window + hubs) * blk, :] = chain(
-                held, lab_bufs.at[t - 1], 1 + t, start_halo)
-            z_down.wait_recv()
-            z_up.wait_recv()
-            pending += [z_down, z_up]
+                held, lab_bufs.at[t - 1], 1 + t, start_halo, hubs)
+            for copy in halo:
+                copy.wait_recv()
+            pending += halo
 
         def apply(m, carry):
             total = jnp.dot(weights[m, :, :span],
@@ -366,21 +378,23 @@
 
     own_rows = own_blocks * blk
 
-    def rows_of(index):
-        return pl.ds(pl.multiple_of(index * own_rows, blk), own_rows)
-
-    last = [
-        remote(res_half.at[rows_of(q_x)], from_x, r_send.at[1], r_recv.at[1], xp),
-        remote(res_half.at[rows_of(q_d)], from_d, r_send.at[2], r_recv.at[2], dp),
-        remote(res.at[rows_of(q_sib)], from_sib, r_send.at[0], r_recv.at[0], sib),
-    ]
+    def result(kind, ref, index, target, device):
+        return [remote(ref.at[pl.ds(pl.multiple_of(index * own_rows + n * blk, blk), blk)],
+                       target.at[n * blk:(n + 1) * blk],
+                       r_send.at[kind, n], r_recv.at[kind, n], device)
+                for n in range(own_blocks)]
+
+    across = result(1, res_half, q_x, from_x, xp) + result(2, res_half, q_d, from_d, dp)
+    beside = result(0, res, q_sib, from_sib, sib)
+    last = across + beside
     there = (1 - x) * (pairs // 2)
     lax.fori_loop(0, pairs // 2, lambda m, carry: apply(there + m, carry), 0)
-    last[0].start()
-    last[1].start()
+    for copy in across:
+        copy.start()
     here = x * (pairs // 2)
     lax.fori_loop(0, pairs // 2, lambda m, carry: apply(here + m, carry), 0)
-    last[2].start()
+    for copy in beside:
+        copy.start()
     for copy in last:
         copy.wait_recv()
     pending += last
@@ -409,11 +423,13 @@
     for to_up, to_down in ends:
         @pl.when(g < groups - 1)
         def _():
-            to_up.wait_send()
+            for copy in to_up:
+                copy.wait_send()
 
         @pl.when(g > 0)
         def _():
-            to_down.wait_send()
+            for copy in to_down:
+                copy.wait_send()
 
 
 def on_device(cols, features, seed_labels, neighbours, hub_blocks):
@@ -471,9 +487,9 @@
             dma((3,)), dma((3,)),
             dma((3,)), dma((3,)),
             dma((2,)), dma((2,)),
-            dma((ITERS + 1, 2)), dma((ITERS + 1, 2)),
-            dma((ITERS - 1, 2)), dma((ITERS - 1, 2)),
-            dma((3,)), dma((3,)),
+            dma((ITERS + 1, 2, GROUP)), dma((ITERS + 1, 2, GROUP)),
+            dma((ITERS - 1, 2, reach)), dma((ITERS - 1, 2, reach)),
+            dma((3, own_blocks)), dma((3, own_blocks)),
         ],
         compiler_params=pltpu.CompilerParams(
             collective_id=0, has_side_effects=True, vmem_limit_bytes=60 * 1024 * 1024),

time: 228 us -> 246 us (1.079)
  Pallas kernels: 222 us -> 240 us
    pallas_call x1, Pallas kernels: 222 us -> 240 us  [on_device(): pl.pallas_call(functools.partial(kernel, groups, blk, cols), out_shape=ja...]
where the time goes in v3:
time: 246 us
  Pallas kernels  240 us (98%)
  local copies, waits for them, and re-layouts  3.56 us (1%)
    pallas_call x1, Pallas kernels, on_device(): pl.pallas_call(functools.partial(kernel, groups, blk, cols), out_shape=ja...  240 us

profile of v3, /device:TPU:1, one launch (start us, length us, event | category | flops | bytes accessed | tf_op | source)
XLA Modules:
  0.0 245.7 jit_solution(13043552181577531284)
XLA Ops:
  0.0 0.8 fusion
  0.8 0.1 convert_reduce_fusion
  0.9 0.7 convert_bitcast_fusion
  1.6 0.6 select_maximum_fusion.meta_ref
  2.2 239.9 %shard_map.46 = f32[640,1024]{1,0:T(8,128)} custom-call(bf16[640,768]{1,0:T(8,128)(2,1)} %feat_ref.1, f32[16,128]{1,0:T(8,128)} %select_maximum_fusion.meta_ref, s32[4]{0:T(128)} %hub_ref.1), custom_call_target="tpu_custom_call" | custom-call | tf_op jit(solution)/shard_map/pallas_call | solution.py:463
  242.1 3.6 %copy.6 = f32[640,1024]{1,0:T(8,128)} copy(f32[640,1024]{1,0:T(8,128)} %shard_map.46) | data formatting | bytes 5242880
  (2 shorter events, 0.0 us)
